TPU v7x, 128 devices: a whole 4x4x4 slice. The times are simulated.
128 devices in a mesh: seq: 16 (over z, y_lo, core), tp: 8 (over x, y_hi).
Axes of the slice: x: 4, y: 4 (y_hi: 2, y_lo: 2; y = y_hi * 2 + y_lo), z: 4, core: 2. Of those that a mesh axis runs over, the one named last changes fastest.
Arguments:
- layer_input: bfloat16 [16, 512, 4096], P('seq')
- memory: bfloat16 [16, 512, 4096], P('seq'), may hold values from -6 to 6
- seg_lengths: int32 [16], replicated, may hold values from 257 to 512, as said below
- query_weight: bfloat16 [4096, 4096], P(None, 'tp')
- key_weight: bfloat16 [4096, 4096], P(None, 'tp')
- value_weight: bfloat16 [4096, 4096], P(None, 'tp'), may hold values from -0.09375 to 0.09375
- out_weight: bfloat16 [4096, 4096], P('tp'), may hold values from -0.1875 to 0.1875
Outputs:
- attended: bfloat16 [16, 512, 4096], P('seq', 'tp')
Inputs may be any that keep to these rules, and one draw needn't show every extreme that they name: `seg_lengths`: slots below a segment's count hold real tokens.
All inputs are finite; a program needn't handle non-finite values.
Results may differ from a plain program's by a relative error of at most 0.011.
Values may be sent and summed in bfloat16 or wider, within the bound.
A program may use at most 128 MiB of HBM per device.

v0:
```python
import math

import jax
import jax.numpy as jnp
from jax import lax
from jax.sharding import PartitionSpec as P

HEAD_DIM = 128


def shifted(x, axis, by):
    devices = lax.axis_size(axis)
    return lax.ppermute(x, axis, [(i, (i + by) % devices) for i in range(devices)])


def cut_along(x, dim, devices):
    before, after = (x.shape[:dim], x.shape[dim + 1 :])
    return jnp.moveaxis(x.reshape(*before, devices, -1, *after), dim, 0)


def sum_at_owner(x, axis, dim):
    devices = lax.axis_size(axis)
    pieces = lax.all_to_all(cut_along(x, dim, devices), axis, 0, 0, tiled=True)
    return jnp.sum(pieces, axis=0)


def project(states, weight):
    return jnp.dot(states, weight, preferred_element_type=jnp.float32).astype(jnp.bfloat16)


def attend_heads(queries, all_keys, all_values, key_ok):
    scores = jnp.einsum(
        "qhd,khd->hqk", queries, all_keys, preferred_element_type=jnp.float32
    ) / math.sqrt(HEAD_DIM)
    row_max = jnp.max(jnp.where(key_ok[None], scores, -1e30), axis=-1, keepdims=True)
    weights = jnp.where(key_ok[None], jnp.exp(scores - row_max), 0.0)
    probabilities = (weights / jnp.sum(weights, axis=-1, keepdims=True)).astype(jnp.bfloat16)
    context = jnp.einsum(
        "hqk,khd->qhd", probabilities, all_values, preferred_element_type=jnp.float32
    )
    return context.astype(jnp.bfloat16)


def body(layer_input, memory, seg_lengths, query_weight, key_weight, value_weight, out_weight):
    seg_count = layer_input.shape[0]
    seg_rows = layer_input.shape[1]
    heads_local = query_weight.shape[1] // HEAD_DIM
    group_index = lax.axis_index("seq")
    seg_total = seg_lengths.shape[0]
    mem_len = lax.dynamic_index_in_dim(
        seg_lengths, jnp.mod(group_index * seg_count - 1, seg_total), 0, keepdims=False
    )
    sent_keys = project(memory[0], key_weight)
    sent_values = project(memory[0], value_weight)
    mem_keys, mem_values = shifted((sent_keys, sent_values), "seq", 1)
    row_ids = jnp.arange(seg_rows, dtype=jnp.int32)[:, None]
    col_ids = jnp.arange(seg_rows, dtype=jnp.int32)[None, :]
    position = group_index * seg_count + 0
    own_len = lax.dynamic_index_in_dim(seg_lengths, position, 0, keepdims=False)
    inputs = layer_input[0]
    queries = project(inputs, query_weight).reshape(seg_rows, heads_local, HEAD_DIM)
    own_keys = project(inputs, key_weight).reshape(seg_rows, heads_local, HEAD_DIM)
    own_values = project(inputs, value_weight).reshape(seg_rows, heads_local, HEAD_DIM)
    mem_ok = jnp.broadcast_to(col_ids < mem_len, (seg_rows, seg_rows))
    own_ok = (col_ids <= row_ids) & (col_ids < own_len)
    key_ok = jnp.concatenate([mem_ok, own_ok], axis=1)
    all_keys = jnp.concatenate(
        [mem_keys.reshape(seg_rows, heads_local, HEAD_DIM), own_keys], axis=0
    )
    all_values = jnp.concatenate(
        [mem_values.reshape(seg_rows, heads_local, HEAD_DIM), own_values], axis=0
    )
    context = attend_heads(queries, all_keys, all_values, key_ok).reshape(
        seg_rows, heads_local * HEAD_DIM
    )
    shared_rows = sum_at_owner(
        jnp.dot(context, out_weight, preferred_element_type=jnp.float32), "tp", 0
    ).astype(jnp.bfloat16)
    pieces = [shared_rows]
    return jnp.stack(pieces)


def solution(mesh):
    return jax.shard_map(
        body,
        mesh=mesh,
        in_specs=(
            P("seq", None, None),
            P("seq", None, None),
            P(),
            P(None, "tp"),
            P(None, "tp"),
            P(None, "tp"),
            P("tp", None),
        ),
        out_specs=P("seq", "tp", None),
        check_vma=False,
    )
```

profile of v0, /device:TPU:0, one launch (start us, length us, event | category | flops | bytes accessed | tf_op | source)
XLA Modules:
  0.0 156.8 jit_solution(6336171848096374949)
XLA Ops:
  0.0 5.9 %fusion.22 = bf16[512,512]{1,0:T(8,128)(2,1)S(1)} fusion(bf16[4096,512]{1,0:T(8,128)(2,1)} %param.12, bf16[1,512,4096]{2,1,0:T(8,128)(2,1)} %param.8), kind=kOutput, calls=%fused_computation.24 | convolution fusion | flops 2147745792 | bytes 8912896 | tf_op jit(solution)/shard_map/dot_general | solution.py:28
  5.9 0.1 collective-permute-start
  6.0 3.1 %fusion.25 = bf16[512,512]{1,0:T(8,128)(2,1)} fusion(bf16[4096,512]{1,0:T(8,128)(2,1)S(1)} %copy-done.2, bf16[1,512,4096]{2,1,0:T(8,128)(2,1)S(1)} %copy-done.1), kind=kOutput, calls=%fused_computation.25 | convolution fusion | flops 2147745792 | bytes 8912896 | tf_op jit(solution)/shard_map/dot_general | solution.py:28
  9.1 1.7 %collective-permute-start.1 = (bf16[512,512]{1,0:T(8,128)(2,1)}, bf16[512,512]{1,0:T(8,128)(2,1)S(1)}, u32[]{:S(2)}, u32[]{:S(2)}) collective-permute-start(bf16[512,512]{1,0:T(8,128)(2,1)} %fusion.25), channel_id=1, source_target_pairs={{0,8},{8,16},{16,24},{24,32},{32,40},{40,48},{48,56},{56,64},{64,7... | collective-permute-start | bytes 1572872 | tf_op jit(solution)/shard_map/ppermute | solution.py:13
  10.9 6.0 %fusion.34 = bf16[512,512]{0,1:T(8,128)(2,1)S(1)} fusion(bf16[4096,512]{1,0:T(8,128)(2,1)} %param.11, bf16[1,512,4096]{2,1,0:T(8,128)(2,1)} %param.7), kind=kOutput, calls=%fused_computation.28 | convolution fusion | flops 2147745792 | bytes 8912896 | tf_op jit(solution)/shard_map/dot_general | solution.py:28
  16.9 0.0 copy-start
  16.9 3.2 %fusion.28 = bf16[512,512]{0,1:T(8,128)(2,1)} fusion(bf16[4096,512]{1,0:T(8,128)(2,1)S(1)} %copy-done.3, bf16[1,512,4096]{2,1,0:T(8,128)(2,1)S(1)} %copy-done.4), kind=kOutput, calls=%fused_computation.26 | convolution fusion | flops 2147745792 | bytes 8912896 | tf_op jit(solution)/shard_map/dot_general | solution.py:28
  20.1 0.6 fusion.52
  20.7 0.6 iota_compare_fusion.2
  21.4 0.6 iota_compare_fusion.1
  21.9 0.1 fusion.43
  22.0 0.3 copy.15
  22.3 0.2 pad_add_fusion
  22.5 6.6 %fusion.31 = bf16[512,512]{0,1:T(8,128)(2,1)} fusion(bf16[4096,512]{1,0:T(8,128)(2,1)} %param.10, bf16[1,512,4096]{2,1,0:T(8,128)(2,1)} %param.7), kind=kOutput, calls=%fused_computation.27 | convolution fusion | flops 2147745792 | bytes 8912896 | tf_op jit(solution)/shard_map/dot_general | solution.py:28
  29.2 0.1 copy_bitcast_fusion
  29.3 9.2 %fusion.53 = (f32[4,512]{1,0:T(4,128)S(1)}, f32[4,512,1024]{2,1,0:T(8,128)}) fusion(pred[512,1024]{1,0:T(8,128)(4,1)S(1)} %pad_add_fusion, bf16[512,4,128]{0,2,1:T(8,128)(2,1)} %bitcast.52, bf16[512,4,128]{2,0,1:T(8,128)(2,1)S(1)} %copy.15, bf16[512,4,128]{2,0,1:T(8,128)(2,1)S(1)} %copy_bitcast_fusion), kind=kOutput, calls=%fused_computation.48 | convolution fusion | flops 1090520064 | bytes 10493952 | tf_op jit(solution)/shard_map/sub | solution.py:36
  38.4 0.0 collective-permute-done
  38.4 0.2 copy.19
  38.6 5.2 %fusion.37 = bf16[512,4,128]{0,2,1:T(8,128)(2,1)S(1)} fusion(f32[4,512,1024]{2,1,0:T(8,128)} %get-tuple-element.8, f32[4,512]{1,0:T(4,128)S(1)} %get-tuple-element.7, bf16[512,4,128]{0,2,1:T(8,128)(2,1)} %bitcast.51, bf16[512,4,128]{0,2,1:T(8,128)(2,1)S(1)} %bitcast.50), kind=kOutput, calls=%fused_computation.29 | convolution fusion | flops 543424512 | bytes 9969664 | tf_op jit(solution)/shard_map/hqk,khd->qhd/dot_general | solution.py:38
  43.8 0.3 copy.17
  44.1 0.2 dot_general.33
  44.3 4.5 %fusion.5 = f32[8,64,4096]{2,1,0:T(8,128)S(1)} fusion(bf16[8,64,512]{2,1,0:T(8,128)(2,1)S(1)} %dot_general.33, bf16[512,4096]{1,0:T(8,128)(2,1)} %param.13), kind=kOutput, calls=%fused_computation.6 | convolution fusion | flops 2147483648 | bytes 13107200 | tf_op jit(solution)/shard_map/dot_general | solution.py:77
  48.9 103.1 %all_to_all.5 = f32[8,64,4096]{2,1,0:T(8,128)} all-to-all(f32[8,64,4096]{2,1,0:T(8,128)S(1)} %fusion.5), channel_id=1, replica_groups=mesh['seq'=16,'tp'=8] {'tp'}, dimensions={0} | all-to-all | bytes 16777216 | tf_op jit(solution)/shard_map/all_to_all | solution.py:23
  152.0 4.8 %reduce_sum.19 = bf16[64,4096]{1,0:T(8,128)(2,1)} reduce(f32[8,64,4096]{2,1,0:T(8,128)} %all_to_all.5, f32[]{:T(128)} %constant.36.clone.1), dimensions={0}, to_apply=%region_2.3 | reduce | flops 1835008 | bytes 8912900 | tf_op jit(solution)/shard_map/reduce_sum | solution.py:24
  (11 shorter events, 0.0 us)
Async XLA Ops:
  0.0 6.0 %copy-start.1 = (bf16[1,512,4096]{2,1,0:T(8,128)(2,1)S(1)}, bf16[1,512,4096]{2,1,0:T(8,128)(2,1)}, u32[]{:S(2)}) copy-start(bf16[1,512,4096]{2,1,0:T(8,128)(2,1)} %param.8) | copy-start | bytes 12582916
  0.0 6.0 %copy-start.2 = (bf16[4096,512]{1,0:T(8,128)(2,1)S(1)}, bf16[4096,512]{1,0:T(8,128)(2,1)}, u32[]{:S(2)}) copy-start(bf16[4096,512]{1,0:T(8,128)(2,1)} %param.11) | copy-start | bytes 12582916
  5.9 32.5 %collective-permute-start = (bf16[512,512]{1,0:T(8,128)(2,1)S(1)}, bf16[512,512]{1,0:T(8,128)(2,1)S(1)}, u32[]{:S(2)}, u32[]{:S(2)}) collective-permute-start(bf16[512,512]{1,0:T(8,128)(2,1)S(1)} %fusion.22), channel_id=1, source_target_pairs={{0,8},{8,16},{16,24},{24,32},{32,40},{40,48},{48,56},{56,64},{64,7... | collective-permute-start | bytes 1572872 | tf_op jit(solution)/shard_map/ppermute | solution.py:13
  9.1 20.0 %collective-permute-start.1 = (bf16[512,512]{1,0:T(8,128)(2,1)}, bf16[512,512]{1,0:T(8,128)(2,1)S(1)}, u32[]{:S(2)}, u32[]{:S(2)}) collective-permute-start(bf16[512,512]{1,0:T(8,128)(2,1)} %fusion.25), channel_id=1, source_target_pairs={{0,8},{8,16},{16,24},{24,32},{32,40},{40,48},{48,56},{56,64},{64,7... | collective-permute-start | bytes 1572872 | tf_op jit(solution)/shard_map/ppermute | solution.py:13
  10.9 6.0 %copy-start.3 = (bf16[4096,512]{1,0:T(8,128)(2,1)S(1)}, bf16[4096,512]{1,0:T(8,128)(2,1)}, u32[]{:S(2)}) copy-start(bf16[4096,512]{1,0:T(8,128)(2,1)} %param.12) | copy-start | bytes 12582916
  10.9 6.0 %copy-start.4 = (bf16[1,512,4096]{2,1,0:T(8,128)(2,1)S(1)}, bf16[1,512,4096]{2,1,0:T(8,128)(2,1)}, u32[]{:S(2)}) copy-start(bf16[1,512,4096]{2,1,0:T(8,128)(2,1)} %param.7) | copy-start | bytes 12582916
  16.9 3.2 %copy-start = (s32[16]{0:T(128)S(1)}, s32[16]{0:T(128)}, u32[]{:S(2)}) copy-start(s32[16]{0:T(128)} %param.9) | copy-start | bytes 196
where the time goes:
time: 157 us
  blocking collectives  103 us (66%)
  matrix products  43.7 us (28%)
  other arithmetic  6.31 us (4%)
  starting transfers between devices  1.82 us (1%)
  local copies, waits for them, and re-layouts  1.69 us (1%)
    all_to_all x1, blocking collectives, sum_at_owner(): pieces = lax.all_to_all(cut_along(x, dim, devices), axis, 0, 0, tiled=True)  103 us
    dot_general x5, matrix products, project(): jnp.dot(states, weight, preferred_element_type=jnp.float32)  24.9 us
    sub x1, matrix products, attend_heads(): weights = jnp.where(key_ok[None], jnp.exp(scores - row_max), 0.0)  9.17 us
    dot_general x1, matrix products, attend_heads(): jnp.einsum('hqk,khd->qhd', probabilities, all_values, preferred_element_t...  5.16 us
    reduce_sum x1, other arithmetic, sum_at_owner(): return jnp.sum(pieces, axis=0)  4.82 us
    dot_general x1, matrix products, body(): jnp.dot(context, out_weight, preferred_element_type=jnp.float32)  4.54 us
  transfers between devices with their start and end apart: 2, of which 0 were waited for; matrix products, arithmetic and copies ran while one was open for 19% of the time, Pallas kernels for 0%

commit v1 on v0

v1 whole, which is shorter than its diff:
```python
import functools
import math

import jax
import jax.numpy as jnp
from jax import lax
from jax.experimental import pallas as pl
from jax.experimental.pallas import tpu as pltpu
from jax.sharding import PartitionSpec as P

F32 = jnp.float32
BF16 = jnp.bfloat16
MESH = pl.DeviceIdType.MESH

SEG = 512
D = 4096
HD = 128
COLS = 512
PAIR = 256
TW = 512
NT = D // TW
Q_SCALE = math.log2(math.e) / math.sqrt(HD)
MASKED = -3e38
D_ORDER = (2, 1, 3, 0)


def kernel(
    lens,
    x_hbm,
    mem_hbm,
    wq_hbm,
    wk_hbm,
    wv_hbm,
    wo_hbm,
    out_ref,
    x_v,
    mem_v,
    w_v,
    wo_v,
    wof,
    kv_send,
    kv_recv,
    own,
    ctx_send,
    ctx_recv,
    ctx_own,
    p_buf,
    r1,
    rb,
    rf,
    ld_sem,
    kvs,
    kvr,
    cxs,
    cxr,
    wcs,
    wcr,
    wzs,
    wzr,
    wbs,
    wbr,
    r1s,
    r1r,
    rbs,
    rbr,
    rfs,
    rfr,
):
    s = lax.axis_index("seq")
    t = lax.axis_index("tp")
    core = lax.rem(s, 2)
    yl = lax.rem(s // 2, 2)
    z = s // 4
    x = t // 2
    yh = lax.rem(t, 2)

    def at(seq, tp):
        return {"seq": seq, "tp": tp}

    following = at(lax.rem(s + 1, 16), t)
    previous = at(lax.rem(s + 15, 16), t)
    partner = at(s, x * 2 + 1 - yh)
    cross = at(z * 4 + (1 - yl) * 2 + core, x * 2 + 1 - yh)
    sibling = at(s + 1 - 2 * core, t)

    def along_z(by):
        return at(lax.rem(z + by + 4, 4) * 4 + yl * 2 + core, t)

    def along_x(by):
        return at(s, lax.rem(x + by + 4, 4) * 2 + yh)

    barrier = pltpu.get_barrier_semaphore()
    for peer in (
        following,
        previous,
        partner,
        cross,
        along_z(1),
        along_z(-1),
        along_x(1),
        along_x(-1),
    ):
        pl.semaphore_signal(barrier, inc=1, device_id=peer, device_id_type=MESH)

    def load_w(src, pair, kind):
        c = pair * 3 + kind
        return pltpu.make_async_copy(
            src.at[:, pl.ds(pair * PAIR, PAIR)], w_v.at[c], ld_sem.at[c]
        )

    load_mem = pltpu.make_async_copy(mem_hbm.at[0], mem_v, ld_sem.at[6])
    load_x = pltpu.make_async_copy(x_hbm.at[0], x_v, ld_sem.at[7])
    load_wo = pltpu.make_async_copy(wo_hbm, wo_v, ld_sem.at[8])
    load_mem.start()
    load_w(wk_hbm, 0, 0).start()
    load_w(wv_hbm, 0, 1).start()
    load_w(wk_hbm, 1, 0).start()
    load_w(wv_hbm, 1, 1).start()
    load_x.start()
    load_w(wq_hbm, 0, 2).start()
    load_w(wq_hbm, 1, 2).start()
    load_wo.start()

    def remote(src, dst, send, recv, to):
        return pltpu.make_async_remote_copy(
            src_ref=src,
            dst_ref=dst,
            send_sem=send,
            recv_sem=recv,
            device_id=to,
            device_id_type=MESH,
        )

    def wait_w(c):
        pltpu.make_async_copy(w_v.at[c], w_v.at[c], ld_sem.at[c]).wait()

    def kv_copy(c):
        return remote(kv_send.at[c], kv_recv.at[c], kvs.at[c], kvr.at[c], following)

    def tile(zz, cc):
        return lax.rem(zz + 4, 4) * 2 + cc

    half = COLS // 2

    def cross_copy(i):
        if i < 2:
            g = tile(z, core)
            rows = pl.ds(i * half, half)
        else:
            g = tile(z + 2, core)
            rows = pl.ds(0, COLS)
        return remote(
            wo_hbm.at[rows, pl.ds(pl.multiple_of(g * TW, TW), TW)],
            wof.at[g, rows],
            wcs.at[i],
            wcr.at[i],
            cross,
        )

    def z_copy(by, i, zz):
        g = tile(zz, core)
        rows = pl.ds(i * half, half)
        k = (1 - by) + i
        return remote(
            wof.at[g, rows], wof.at[g, rows], wzs.at[k], wzr.at[k], along_z(by)
        )

    def sibling_copy(i, cc):
        g = tile(z + (0, 1, -1, 2)[i], cc)
        return remote(wof.at[g], wof.at[g], wbs.at[i], wbr.at[i], sibling)

    load_mem.wait()

    def mem_step(c, _):
        w = c + c // 2
        wait_w(w)
        kv_send[c] = jnp.dot(mem_v[...], w_v[w], preferred_element_type=F32).astype(BF16)

        @pl.when(c == 0)
        def _():
            pl.semaphore_wait(barrier, 8)
            for i in range(3):
                cross_copy(i).start()

        kv_copy(c).start()
        return 0

    lax.fori_loop(0, 4, mem_step, 0)
    load_x.wait()

    own_len = lens[s]
    mem_len = lens[lax.rem(s + 15, 16)]

    def row_start(d, which):
        return (lax.rem(x + d, 4) * 2 + which) * 64

    def attend(pair, which, dst):
        rows = [pl.ds(pl.multiple_of(row_start(d, which), 64), 64) for d in D_ORDER]
        ids = jnp.concatenate(
            [
                lax.broadcasted_iota(jnp.int32, (64, 1), 0) + row_start(d, which)
                for d in D_ORDER
            ],
            axis=0,
        )
        last = jnp.minimum(ids, own_len - 1)
        col = lax.broadcasted_iota(jnp.int32, (1, SEG), 1)
        ones = jnp.ones((SEG, HD), BF16)
        for hh in range(2):
            cs = slice(hh * HD, (hh + 1) * HD)
            q = jnp.concatenate([own[pair * 3 + 2, r, cs] for r in rows], axis=0)
            dims = (((1,), (1,)), ((), ()))
            s_mem = lax.dot_general(
                q, kv_recv[pair * 2, :, cs], dims, preferred_element_type=F32
            )
            s_own = lax.dot_general(
                q, own[pair * 3, :, cs], dims, preferred_element_type=F32
            )
            s_mem = jnp.where(col < mem_len, s_mem, MASKED)
            s_own = jnp.where(col <= last, s_own, MASKED)
            top = jnp.max(jnp.maximum(s_mem, s_own), axis=1, keepdims=True)
            w_mem = jnp.exp2(s_mem - top).astype(BF16)
            w_own = jnp.exp2(s_own - top).astype(BF16)
            v_mem = jnp.concatenate([kv_recv[pair * 2 + 1, :, cs], ones], axis=1)
            v_own = jnp.concatenate([own[pair * 3 + 1, :, cs], ones], axis=1)
            r = jnp.dot(w_mem, v_mem, preferred_element_type=F32) + jnp.dot(
                w_own, v_own, preferred_element_type=F32
            )
            dst[pair, :, cs] = (r[:, :HD] / r[:, HD:]).astype(BF16)

    def ctx_copy(pair, i):
        rows = pl.ds(i * 128, 128)
        k = pair * 2 + i
        return remote(
            ctx_send.at[pair, rows], ctx_recv.at[pair, rows], cxs.at[k], cxr.at[k], partner
        )

    def own_step(c, _):
        pair = c // 3

        @pl.when(lax.rem(c, 3) == 2)
        def _():
            wait_w(c)

        scale = jnp.where(lax.rem(c, 3) == 2, Q_SCALE, 1.0).astype(F32)
        own[c] = (
            jnp.dot(x_v[...], w_v[c], preferred_element_type=F32) * scale
        ).astype(BF16)

        @pl.when(c == 2)
        def _():
            cross_copy(0).wait_recv()
            z_copy(1, 0, z).start()
            z_copy(-1, 0, z).start()

        @pl.when(c == 4)
        def _():
            cross_copy(1).wait_recv()
            z_copy(1, 1, z).start()
            z_copy(-1, 1, z).start()
            sibling_copy(0, core).start()

        @pl.when(lax.rem(c, 3) == 2)
        def _():
            kv_copy(pair * 2).wait_recv()
            kv_copy(pair * 2 + 1).wait_recv()
            attend(pair, 1 - yh, ctx_send)
            ctx_copy(pair, 0).start()
            ctx_copy(pair, 1).start()
            attend(pair, yh, ctx_own)

        return 0

    lax.fori_loop(0, 6, own_step, 0)
    load_wo.wait()
    for pair in range(2):
        for i in range(2):
            ctx_copy(pair, i).wait_recv()

    def tile_of(k):
        j = k // 2
        off = j + j // 2 - 2 * (j // 3)
        par = lax.rem(k, 2)
        return tile(z + off, core + par * (1 - 2 * core))

    def far_copy(k):
        sgn = 1 - 2 * lax.rem(k, 2)
        return remote(
            p_buf.at[k, pl.ds(0, 64)], r1.at[k], r1s.at[k], r1r.at[k], along_x(sgn)
        )

    def back_copy(k):
        par = lax.rem(k, 2)
        rows = pl.ds(pl.multiple_of(128 - 64 * par, 64), 64)
        return remote(
            p_buf.at[k, rows], rb.at[k], rbs.at[k], rbr.at[k], along_x(2 * par - 1)
        )

    def fwd_rows(k):
        return pl.ds(pl.multiple_of(64 + 64 * lax.rem(k, 2), 64), 64)

    def fwd_copy(k):
        return remote(
            p_buf.at[k, fwd_rows(k)],
            rf.at[k],
            rfs.at[k],
            rfr.at[k],
            along_x(1 - 2 * lax.rem(k, 2)),
        )

    def project_tile(k):
        g = tile_of(k)
        cols = pl.ds(pl.multiple_of(g * TW, TW), TW)
        acc = jnp.dot(ctx_own[0], wo_v[0:PAIR, cols], preferred_element_type=F32)
        acc += jnp.dot(ctx_own[1], wo_v[PAIR:COLS, cols], preferred_element_type=F32)
        acc += jnp.dot(ctx_recv[0], wof[g, 0:PAIR], preferred_element_type=F32)
        acc += jnp.dot(ctx_recv[1], wof[g, PAIR:COLS], preferred_element_type=F32)
        p_buf[k] = acc.astype(BF16)
        far_copy(k).start()
        back_copy(k).start()

    def combine(k):
        far_copy(k).wait_recv()
        rows = fwd_rows(k)
        p_buf[k, rows] = (p_buf[k, rows].astype(F32) + r1[k].astype(F32)).astype(BF16)
        fwd_copy(k).start()

    def finish(k):
        back_copy(k).wait_recv()
        fwd_copy(k).wait_recv()
        g = tile_of(k)
        cols = pl.ds(pl.multiple_of(g * TW, TW), TW)
        out_ref[:, cols] = (
            p_buf[k, 192:256].astype(F32) + rb[k].astype(F32) + rf[k].astype(F32)
        ).astype(BF16)

    def out_step(k, _):
        for j in range(4):

            @pl.when(k == 2 * j)
            def _(j=j):
                if j == 1:
                    z_copy(-1, 0, z + 1).wait_recv()
                    z_copy(-1, 1, z + 1).wait_recv()
                if j == 2:
                    z_copy(1, 0, z - 1).wait_recv()
                    z_copy(1, 1, z - 1).wait_recv()
                if j == 3:
                    cross_copy(2).wait_recv()
                if j > 0:
                    sibling_copy(j, core).start()

            @pl.when(k == 2 * j + 1)
            def _(j=j):
                sibling_copy(j, 1 - core).wait_recv()

        @pl.when(k < NT)
        def _():
            project_tile(k)

        @pl.when(k >= 2)
        def _():
            combine(k - 2)

        return 0

    lax.fori_loop(0, NT + 2, out_step, 0)

    def last_step(k, _):
        finish(k)
        return 0

    lax.fori_loop(0, NT, last_step, 0)

    for c in range(4):
        kv_copy(c).wait_send()
        sibling_copy(c, core).wait_send()
        ctx_copy(c // 2, c % 2).wait_send()
    for i in range(3):
        cross_copy(i).wait_send()
    for i in range(2):
        z_copy(1, i, z).wait_send()
        z_copy(-1, i, z).wait_send()

    def drain(k, _):
        far_copy(k).wait_send()
        back_copy(k).wait_send()
        fwd_copy(k).wait_send()
        return 0

    lax.fori_loop(0, NT, drain, 0)


def body(layer_input, memory, seg_lengths, query_weight, key_weight, value_weight, out_weight):
    dma = pltpu.SemaphoreType.DMA
    out = pl.pallas_call(
        kernel,
        out_shape=jax.ShapeDtypeStruct((64, D), BF16),
        in_specs=[pl.BlockSpec(memory_space=pltpu.SMEM)]
        + [pl.BlockSpec(memory_space=pl.ANY)] * 6,
        out_specs=pl.BlockSpec(memory_space=pltpu.VMEM),
        scratch_shapes=[
            pltpu.VMEM((SEG, D), BF16),
            pltpu.VMEM((SEG, D), BF16),
            pltpu.VMEM((6, D, PAIR), BF16),
            pltpu.VMEM((COLS, D), BF16),
            pltpu.VMEM((NT, COLS, TW), BF16),
            pltpu.VMEM((4, SEG, PAIR), BF16),
            pltpu.VMEM((4, SEG, PAIR), BF16),
            pltpu.VMEM((6, SEG, PAIR), BF16),
            pltpu.VMEM((2, 256, PAIR), BF16),
            pltpu.VMEM((2, 256, PAIR), BF16),
            pltpu.VMEM((2, 256, PAIR), BF16),
            pltpu.VMEM((NT, 256, TW), BF16),
            pltpu.VMEM((NT, 64, TW), BF16),
            pltpu.VMEM((NT, 64, TW), BF16),
            pltpu.VMEM((NT, 64, TW), BF16),
            dma((9,)),
            dma((4,)),
            dma((4,)),
            dma((4,)),
            dma((4,)),
            dma((3,)),
            dma((3,)),
            dma((4,)),
            dma((4,)),
            dma((4,)),
            dma((4,)),
            dma((NT,)),
            dma((NT,)),
            dma((NT,)),
            dma((NT,)),
            dma((NT,)),
            dma((NT,)),
        ],
        compiler_params=pltpu.CompilerParams(
            collective_id=0, has_side_effects=True, vmem_limit_bytes=60 * 2**20
        ),
    )(
        seg_lengths,
        layer_input,
        memory,
        query_weight,
        key_weight,
        value_weight,
        out_weight,
    )
    return out[None]


def solution(mesh):
    return jax.shard_map(
        body,
        mesh=mesh,
        in_specs=(
            P("seq", None, None),
            P("seq", None, None),
            P(),
            P(None, "tp"),
            P(None, "tp"),
            P(None, "tp"),
            P("tp", None),
        ),
        out_specs=P("seq", "tp", None),
        check_vma=False,
    )
```

time: 157 us -> 54.1 us (0.34)
  blocking collectives: 103 us -> 0 us
  Pallas kernels: 0 us -> 52.1 us
  matrix products: 43.7 us -> 0 us
  other arithmetic: 6.31 us -> 0 us
  starting transfers between devices: 1.82 us -> 0 us
    all_to_all x1 -> x0, blocking collectives: 103 us -> none  [sum_at_owner(): pieces = lax.all_to_all(cut_along(x, dim, devices), axis, 0, 0, tiled=True)]
    pallas_call x0 -> x1, Pallas kernels: none -> 52.1 us  [body(): pl.pallas_call(kernel, out_shape=jax.ShapeDtypeStruct((64, D), BF16), in_...]
    dot_general x7 -> x0, matrix products: 34.6 us -> none  [the longest x5 24.9 us: project(): jnp.dot(states, weight, preferred_element_type=jnp.float32)]
    sub x1 -> x0, matrix products: 9.17 us -> none  [attend_heads(): weights = jnp.where(key_ok[None], jnp.exp(scores - row_max), 0.0)]
    reduce_sum x1 -> x0, other arithmetic: 4.82 us -> none  [sum_at_owner(): return jnp.sum(pieces, axis=0)]
    unnamed x10 -> x1, local copies, waits for them, and re-layouts: 0.02 us -> 1.87 us
    ppermute x2 -> x0, starting transfers between devices: 1.82 us -> none  [shifted(): lax.ppermute(x, axis, [(i, (i + by) % devices) for i in range(devices)])]
  transfers between devices with their start and end apart: 2 -> 0, of which waited for: 0 -> 0; matrix products, arithmetic and copies ran while one was open for 19% -> 0% of each run, Pallas kernels for 0% -> 0%
where the time goes in v1:
time: 54.1 us; the launch traced here: 54 us
  Pallas kernels  52.1 us (96%)
  local copies, waits for them, and re-layouts  1.87 us (3%)
    pallas_call x1, Pallas kernels, body(): pl.pallas_call(kernel, out_shape=jax.ShapeDtypeStruct((64, D), BF16), in_...  52.1 us
    unnamed x1, local copies, waits for them, and re-layouts  1.87 us

profile of v1, /device:TPU:0, one launch (start us, length us, event | category | flops | bytes accessed | tf_op | source)
XLA Modules:
  0.0 54.0 jit_solution(9051503512072836908)
XLA Ops:
  0.0 52.1 %shard_map.73 = bf16[64,4096]{1,0:T(8,128)(2,1)} custom-call(s32[16]{0:T(128)} %lens.1, bf16[1,512,4096]{2,1,0:T(8,128)(2,1)} %x_hbm.1, bf16[1,512,4096]{2,1,0:T(8,128)(2,1)} %mem_hbm.1, bf16[4096,512]{1,0:T(8,128)(2,1)} %wq_hbm.1, bf16[4096,512]{1,0:T(8,128)(2,1)} %wk_hbm.1, bf16[4096,512]{1,0:T(8,128)(2,1)} %wv_hbm.1, bf16[512,4096]{1,0:T(8,128)(2,1)} %wo_hbm.1), custom_call_target="tpu_custom_call" | custom-call | tf_op jit(solution)/shard_map/pallas_call | solution.py:396
  52.1 1.9 %copy.9 = bf16[1,64,4096]{2,1,0:T(8,128)(2,1)} copy(bf16[1,64,4096]{2,1,0:T(8,128)(2,1)} %bitcast.1) | data formatting | bytes 1048576

commit v2 on v1

v2 whole, which is shorter than its diff:
```python
import functools
import math

import jax
import jax.numpy as jnp
from jax import lax
from jax.experimental import pallas as pl
from jax.experimental.pallas import tpu as pltpu
from jax.sharding import PartitionSpec as P

F32 = jnp.float32
BF16 = jnp.bfloat16
MESH = pl.DeviceIdType.MESH

SEG = 512
D = 4096
HD = 128
COLS = 512
PAIR = 256
PART = 1024
TW = 512
NT = D // TW
SCALE = math.log2(math.e) / math.sqrt(HD)
MASKED = -3e38
D_ORDER = (2, 1, 3, 0)


def kernel(
    lens,
    x_hbm,
    mem_hbm,
    wq_hbm,
    wk_hbm,
    wv_hbm,
    wo_hbm,
    out_ref,
    states,
    w_v,
    wo_v,
    wof,
    kv_send,
    kv_recv,
    made,
    ctx,
    ctx_recv,
    first,
    p_loc,
    p_buf,
    r1,
    rb,
    rf,
    ld_sem,
    kvs,
    kvr,
    cxs,
    cxr,
    wcs,
    wcr,
    wzs,
    wzr,
    wbs,
    wbr,
    r1s,
    r1r,
    rbs,
    rbr,
    rfs,
    rfr,
):
    s = lax.axis_index("seq")
    t = lax.axis_index("tp")
    core = lax.rem(s, 2)
    yl = lax.rem(s // 2, 2)
    z = s // 4
    x = t // 2
    yh = lax.rem(t, 2)

    def at(seq, tp):
        return {"seq": seq, "tp": tp}

    following = at(lax.rem(s + 1, 16), t)
    previous = at(lax.rem(s + 15, 16), t)
    partner = at(s, x * 2 + 1 - yh)
    cross = at(z * 4 + (1 - yl) * 2 + core, x * 2 + 1 - yh)
    sibling = at(s + 1 - 2 * core, t)

    def along_z(by):
        return at(lax.rem(z + by + 4, 4) * 4 + yl * 2 + core, t)

    def along_x(by):
        return at(s, lax.rem(x + by + 4, 4) * 2 + yh)

    barrier = pltpu.get_barrier_semaphore()
    for peer in (
        following,
        previous,
        partner,
        cross,
        along_z(1),
        along_z(-1),
        along_x(1),
        along_x(-1),
    ):
        pl.semaphore_signal(barrier, inc=1, device_id=peer, device_id_type=MESH)

    def load_w(src, pair, kind, part, depth, sem):
        rows = pl.ds(part * depth, depth)
        return pltpu.make_async_copy(
            src.at[rows, pl.ds(pair * PAIR, PAIR)],
            w_v.at[pair, rows, pl.ds(kind * PAIR, PAIR)],
            ld_sem.at[sem],
        )

    def first_loads(i):
        part = pl.ds(pl.multiple_of(i * PART, PART), PART)
        return (
            pltpu.make_async_copy(
                mem_hbm.at[0, :, part], states.at[0, :, part], ld_sem.at[i]
            ),
            load_w(wk_hbm, 0, 0, i, PART, 4 + i),
        )

    load_v0 = load_w(wv_hbm, 0, 1, 0, D, 8)

    load_kv1 = (
        load_w(wk_hbm, 1, 0, 0, D, 12),
        load_w(wv_hbm, 1, 1, 0, D, 13),
    )
    load_x = pltpu.make_async_copy(x_hbm.at[0], states.at[1], ld_sem.at[14])
    load_q = pltpu.make_async_copy(wq_hbm, w_v.at[2], ld_sem.at[15])
    load_wo = pltpu.make_async_copy(wo_hbm, wo_v, ld_sem.at[16])
    for i in range(2):
        for copy in first_loads(i):
            copy.start()

    def remote(src, dst, send, recv, to):
        return pltpu.make_async_remote_copy(
            src_ref=src,
            dst_ref=dst,
            send_sem=send,
            recv_sem=recv,
            device_id=to,
            device_id_type=MESH,
        )

    def kv_copy(c):
        return remote(kv_send.at[c], kv_recv.at[c], kvs.at[c], kvr.at[c], following)

    def tile(zz, cc):
        return lax.rem(zz + 4, 4) * 2 + cc

    half = COLS // 2

    def cross_copy(i):
        g = tile(z + 2 * (i // 2), core)
        rows = pl.ds((i % 2) * half, half)
        return remote(
            wo_hbm.at[rows, pl.ds(pl.multiple_of(g * TW, TW), TW)],
            wof.at[g, rows],
            wcs.at[i],
            wcr.at[i],
            cross,
        )

    def z_copy(by, i, zz):
        g = tile(zz, core)
        rows = pl.ds(i * half, half)
        k = (1 - by) + i
        return remote(
            wof.at[g, rows], wof.at[g, rows], wzs.at[k], wzr.at[k], along_z(by)
        )

    def sibling_copy(i, cc):
        g = tile(z + (0, 1, -1, 2)[i], cc)
        return remote(wof.at[g], wof.at[g], wbs.at[i], wbr.at[i], sibling)

    own_len = lens[s]
    mem_len = lens[lax.rem(s + 15, 16)]

    def row_start(d, which):
        return (lax.rem(x + d, 4) * 2 + which) * 64

    def at_column(c):
        return c if isinstance(c, int) else pl.multiple_of(c, HD)

    def attend(pairs, group):
        which = 1 - yh + group * (2 * yh - 1)
        starts = [row_start(d, which) for d in D_ORDER]
        rows = [pl.ds(pl.multiple_of(start, 64), 64) for start in starts]
        ids = jnp.concatenate(
            [lax.broadcasted_iota(jnp.int32, (64, 1), 0) + start for start in starts],
            axis=0,
        )
        last = jnp.minimum(ids, own_len - 1)
        col = lax.broadcasted_iota(jnp.int32, (1, SEG), 1)
        ones = jnp.ones((SEG, HD), BF16)
        for pair, hh in [(pair, hh) for pair in pairs for hh in range(2)]:
            ks = slice(hh * HD, (hh + 1) * HD)
            vs = slice(PAIR + hh * HD, PAIR + (hh + 1) * HD)
            qs = pl.ds(at_column(pair * PAIR + hh * HD), HD)
            q = jnp.concatenate([made[2, r, qs] for r in rows], axis=0)
            dims = (((1,), (1,)), ((), ()))
            s_mem = SCALE * lax.dot_general(
                q, kv_recv[2 * pair, :, ks], dims, preferred_element_type=F32
            )
            s_own = SCALE * lax.dot_general(
                q, made[3 + pair, :, ks], dims, preferred_element_type=F32
            )
            s_mem = jnp.concatenate(
                [
                    s_mem[:, :256],
                    jnp.where(col[:, 256:] < mem_len, s_mem[:, 256:], MASKED),
                ],
                axis=1,
            )
            s_own = jnp.where(col <= last, s_own, MASKED)
            top = jnp.max(jnp.maximum(s_mem, s_own), axis=1, keepdims=True)
            w_mem = jnp.exp2(s_mem - top).astype(BF16)
            w_own = jnp.exp2(s_own - top).astype(BF16)
            v_mem = jnp.concatenate([kv_recv[2 * pair + 1, :, ks], ones], axis=1)
            v_own = jnp.concatenate([made[3 + pair, :, vs], ones], axis=1)
            r = jnp.dot(w_mem, v_mem, preferred_element_type=F32) + jnp.dot(
                w_own, v_own, preferred_element_type=F32
            )
            ctx[group * 2 + pair, :, ks] = (r[:, :HD] / r[:, HD:]).astype(BF16)

    def ctx_copy(pair):
        return remote(
            ctx.at[pair], ctx_recv.at[pair], cxs.at[pair], cxr.at[pair], partner
        )

    def first_part(i, _):
        c = i // 4
        n = lax.rem(i, 4)

        @pl.when(i < 4)
        def _():
            for copy in first_loads(n):
                copy.wait()

        @pl.when(i < 2)
        def _():
            for copy in first_loads(n + 2):
                copy.start()

        @pl.when(i == 2)
        def _():
            load_v0.start()

        @pl.when(i == 4)
        def _():
            load_v0.wait()
            load_kv1[0].start()
            load_kv1[1].start()

        part = pl.ds(pl.multiple_of(n * PART, PART), PART)
        cols = pl.ds(pl.multiple_of(c * PAIR, PAIR), PAIR)
        term = jnp.dot(
            states[0, :, part], w_v[0, part, cols], preferred_element_type=F32
        )

        @pl.when(n == 0)
        def _():
            first[...] = term

        @pl.when(n > 0)
        def _():
            first[...] += term

        @pl.when(n == 3)
        def _():
            kv_send[c] = first[...].astype(BF16)

        @pl.when(i == 3)
        def _():
            pl.semaphore_wait(barrier, 8)

        @pl.when(n == 3)
        def _():
            kv_copy(c).start()

        @pl.when(i == 3)
        def _():
            cross_copy(0).start()
            cross_copy(1).start()

        return 0

    lax.fori_loop(0, 8, first_part, 0)

    def make(i, _):
        own_part = jnp.minimum(i // 2, 1)
        w = lax.rem(i, 3)

        @pl.when(i == 1)
        def _():
            load_x.start()
            load_q.start()
            load_kv1[0].wait()
            load_kv1[1].wait()

        @pl.when(i == 2)
        def _():
            load_x.wait()
            load_q.wait()
            load_wo.start()

        made[i] = jnp.dot(
            states[own_part], w_v[w], preferred_element_type=F32
        ).astype(BF16)

        @pl.when(i == 1)
        def _():
            for c in range(2):
                kv_send[2 + c] = made[1, :, c * PAIR : (c + 1) * PAIR]
                kv_copy(2 + c).start()

        @pl.when(i == 3)
        def _():
            cross_copy(0).wait_recv()
            z_copy(1, 0, z).start()
            z_copy(-1, 0, z).start()

        @pl.when(i == 4)
        def _():
            cross_copy(1).wait_recv()
            z_copy(1, 1, z).start()
            z_copy(-1, 1, z).start()
            sibling_copy(0, core).start()
            cross_copy(2).start()

        return 0

    def phase(ph, _):
        lax.fori_loop(1 + 3 * ph, 4 + ph, make, 0)
        kv_copy(2 * ph).wait_recv()
        kv_copy(2 * ph + 1).wait_recv()
        attend((ph,), 0)
        ctx_copy(ph).start()
        return 0

    lax.fori_loop(0, 2, phase, 0)
    cross_copy(3).start()
    attend((0, 1), 1)
    load_wo.wait()

    def both_pairs(ref, at_pair):
        return jnp.concatenate([ref[at_pair], ref[at_pair + 1]], axis=1)

    def local_step(i, _):
        cols = pl.ds(pl.multiple_of(i * 1024, 1024), 1024)
        p_loc[:, cols] = jnp.dot(
            both_pairs(ctx, 2), wo_v[:, cols], preferred_element_type=F32
        )
        return 0

    lax.fori_loop(0, 4, local_step, 0)
    ctx_copy(0).wait_recv()
    ctx_copy(1).wait_recv()

    def tile_of(k):
        j = k // 2
        off = j + j // 2 - 2 * (j // 3)
        par = lax.rem(k, 2)
        return tile(z + off, core + par * (1 - 2 * core))

    def far_copy(k):
        sgn = 1 - 2 * lax.rem(k, 2)
        return remote(
            p_buf.at[k, pl.ds(0, 64)], r1.at[k], r1s.at[k], r1r.at[k], along_x(sgn)
        )

    def back_copy(k):
        par = lax.rem(k, 2)
        rows = pl.ds(pl.multiple_of(128 - 64 * par, 64), 64)
        return remote(
            p_buf.at[k, rows], rb.at[k], rbs.at[k], rbr.at[k], along_x(2 * par - 1)
        )

    def fwd_rows(k):
        return pl.ds(pl.multiple_of(64 + 64 * lax.rem(k, 2), 64), 64)

    def fwd_copy(k):
        return remote(
            p_buf.at[k, fwd_rows(k)],
            rf.at[k],
            rfs.at[k],
            rfr.at[k],
            along_x(1 - 2 * lax.rem(k, 2)),
        )

    def project_tile(k):
        g = tile_of(k)
        cols = pl.ds(pl.multiple_of(g * TW, TW), TW)
        acc = p_loc[:, cols] + jnp.dot(
            both_pairs(ctx_recv, 0), wof[g], preferred_element_type=F32
        )
        p_buf[k] = acc.astype(BF16)
        far_copy(k).start()
        back_copy(k).start()

    def combine(k):
        far_copy(k).wait_recv()
        rows = fwd_rows(k)
        p_buf[k, rows] = (p_buf[k, rows].astype(F32) + r1[k].astype(F32)).astype(BF16)
        fwd_copy(k).start()

    def finish(k):
        back_copy(k).wait_recv()
        fwd_copy(k).wait_recv()
        g = tile_of(k)
        cols = pl.ds(pl.multiple_of(g * TW, TW), TW)
        out_ref[:, cols] = (
            p_buf[k, 192:256].astype(F32) + rb[k].astype(F32) + rf[k].astype(F32)
        ).astype(BF16)

    def out_step(k, _):
        for j in range(4):

            @pl.when(k == 2 * j)
            def _(j=j):
                if j == 1:
                    z_copy(-1, 0, z + 1).wait_recv()
                    z_copy(-1, 1, z + 1).wait_recv()
                if j == 2:
                    z_copy(1, 0, z - 1).wait_recv()
                    z_copy(1, 1, z - 1).wait_recv()
                if j == 3:
                    cross_copy(2).wait_recv()
                    cross_copy(3).wait_recv()
                if j > 0:
                    sibling_copy(j, core).start()

            @pl.when(k == 2 * j + 1)
            def _(j=j):
                sibling_copy(j, 1 - core).wait_recv()

        @pl.when(k < NT)
        def _():
            project_tile(k)

        @pl.when(k >= 4)
        def _():
            combine(k - 4)

        return 0

    lax.fori_loop(0, NT + 4, out_step, 0)

    def last_step(k, _):
        finish(k)
        return 0

    lax.fori_loop(0, NT, last_step, 0)

    for c in range(4):
        sibling_copy(c, core).wait_send()
        cross_copy(c).wait_send()
        kv_copy(c).wait_send()
    for pair in range(2):
        ctx_copy(pair).wait_send()
    for i in range(2):
        z_copy(1, i, z).wait_send()
        z_copy(-1, i, z).wait_send()

    def drain(k, _):
        far_copy(k).wait_send()
        back_copy(k).wait_send()
        fwd_copy(k).wait_send()
        return 0

    lax.fori_loop(0, NT, drain, 0)


def body(layer_input, memory, seg_lengths, query_weight, key_weight, value_weight, out_weight):
    dma = pltpu.SemaphoreType.DMA
    out = pl.pallas_call(
        kernel,
        out_shape=jax.ShapeDtypeStruct((64, D), BF16),
        in_specs=[pl.BlockSpec(memory_space=pltpu.SMEM)]
        + [pl.BlockSpec(memory_space=pl.ANY)] * 6,
        out_specs=pl.BlockSpec(memory_space=pltpu.VMEM),
        scratch_shapes=[
            pltpu.VMEM((2, SEG, D), BF16),
            pltpu.VMEM((3, D, COLS), BF16),
            pltpu.VMEM((COLS, D), BF16),
            pltpu.VMEM((NT, COLS, TW), BF16),
            pltpu.VMEM((4, SEG, PAIR), BF16),
            pltpu.VMEM((4, SEG, PAIR), BF16),
            pltpu.VMEM((5, SEG, COLS), BF16),
            pltpu.VMEM((4, 256, PAIR), BF16),
            pltpu.VMEM((2, 256, PAIR), BF16),
            pltpu.VMEM((SEG, PAIR), F32),
            pltpu.VMEM((256, D), F32),
            pltpu.VMEM((NT, 256, TW), BF16),
            pltpu.VMEM((NT, 64, TW), BF16),
            pltpu.VMEM((NT, 64, TW), BF16),
            pltpu.VMEM((NT, 64, TW), BF16),
            dma((17,)),
            dma((4,)),
            dma((4,)),
            dma((2,)),
            dma((2,)),
            dma((4,)),
            dma((4,)),
            dma((4,)),
            dma((4,)),
            dma((4,)),
            dma((4,)),
            dma((NT,)),
            dma((NT,)),
            dma((NT,)),
            dma((NT,)),
            dma((NT,)),
            dma((NT,)),
        ],
        compiler_params=pltpu.CompilerParams(
            collective_id=0, has_side_effects=True, vmem_limit_bytes=60 * 2**20
        ),
    )(
        seg_lengths,
        layer_input,
        memory,
        query_weight,
        key_weight,
        value_weight,
        out_weight,
    )
    return out[None]


def solution(mesh):
    return jax.shard_map(
        body,
        mesh=mesh,
        in_specs=(
            P("seq", None, None),
            P("seq", None, None),
            P(),
            P(None, "tp"),
            P(None, "tp"),
            P(None, "tp"),
            P("tp", None),
        ),
        out_specs=P("seq", "tp", None),
        check_vma=False,
    )
```

time: 54.1 us -> 52.7 us (0.974)
  Pallas kernels: 52.1 us -> 50.3 us
    pallas_call x1, Pallas kernels: 52.1 us -> 50.3 us  [body(): pl.pallas_call(kernel, out_shape=jax.ShapeDtypeStruct((64, D), BF16), in_...]
where the time goes in v2:
time: 52.7 us; the launch traced here: 52.1 us
  Pallas kernels  50.3 us (95%)
  local copies, waits for them, and re-layouts  1.87 us (4%)
    pallas_call x1, Pallas kernels, body(): pl.pallas_call(kernel, out_shape=jax.ShapeDtypeStruct((64, D), BF16), in_...  50.3 us
    unnamed x1, local copies, waits for them, and re-layouts  1.87 us

profile of v2, /device:TPU:0, one launch (start us, length us, event | category | flops | bytes accessed | tf_op | source)
XLA Modules:
  0.0 52.1 jit_solution(15641849659077881071)
XLA Ops:
  0.0 50.3 %shard_map.73 = bf16[64,4096]{1,0:T(8,128)(2,1)} custom-call(s32[16]{0:T(128)} %lens.1, bf16[1,512,4096]{2,1,0:T(8,128)(2,1)} %x_hbm.1, bf16[1,512,4096]{2,1,0:T(8,128)(2,1)} %mem_hbm.1, bf16[4096,512]{1,0:T(8,128)(2,1)} %wq_hbm.1, bf16[4096,512]{1,0:T(8,128)(2,1)} %wk_hbm.1, bf16[4096,512]{1,0:T(8,128)(2,1)} %wv_hbm.1, bf16[512,4096]{1,0:T(8,128)(2,1)} %wo_hbm.1), custom_call_target="tpu_custom_call" | custom-call | tf_op jit(solution)/shard_map/pallas_call | solution.py:477
  50.3 1.9 %copy.9 = bf16[1,64,4096]{2,1,0:T(8,128)(2,1)} copy(bf16[1,64,4096]{2,1,0:T(8,128)(2,1)} %bitcast.1) | data formatting | bytes 1048576

commit v3 on v2

--- a/solution.py
+++ b/solution.py
@@ -26,7 +26,7 @@
 
 
 def kernel(
-    lens,
+    lens_hbm,
     x_hbm,
     mem_hbm,
     wq_hbm,
@@ -34,6 +34,7 @@
     wv_hbm,
     wo_hbm,
     out_ref,
+    lens,
     states,
     w_v,
     wo_v,
@@ -126,12 +127,14 @@
         load_w(wk_hbm, 1, 0, 0, D, 12),
         load_w(wv_hbm, 1, 1, 0, D, 13),
     )
+    load_lens = pltpu.make_async_copy(lens_hbm, lens, ld_sem.at[17])
     load_x = pltpu.make_async_copy(x_hbm.at[0], states.at[1], ld_sem.at[14])
     load_q = pltpu.make_async_copy(wq_hbm, w_v.at[2], ld_sem.at[15])
     load_wo = pltpu.make_async_copy(wo_hbm, wo_v, ld_sem.at[16])
     for i in range(2):
         for copy in first_loads(i):
             copy.start()
+    load_lens.start()
 
     def remote(src, dst, send, recv, to):
         return pltpu.make_async_remote_copy(
@@ -174,6 +177,7 @@
         g = tile(z + (0, 1, -1, 2)[i], cc)
         return remote(wof.at[g], wof.at[g], wbs.at[i], wbr.at[i], sibling)
 
+    load_lens.wait()
     own_len = lens[s]
     mem_len = lens[lax.rem(s + 15, 16)]
 
@@ -477,10 +481,10 @@
     out = pl.pallas_call(
         kernel,
         out_shape=jax.ShapeDtypeStruct((64, D), BF16),
-        in_specs=[pl.BlockSpec(memory_space=pltpu.SMEM)]
-        + [pl.BlockSpec(memory_space=pl.ANY)] * 6,
+        in_specs=[pl.BlockSpec(memory_space=pltpu.HBM)] * 7,
         out_specs=pl.BlockSpec(memory_space=pltpu.VMEM),
         scratch_shapes=[
+            pltpu.SMEM((16,), jnp.int32),
             pltpu.VMEM((2, SEG, D), BF16),
             pltpu.VMEM((3, D, COLS), BF16),
             pltpu.VMEM((COLS, D), BF16),
@@ -496,7 +500,7 @@
             pltpu.VMEM((NT, 64, TW), BF16),
             pltpu.VMEM((NT, 64, TW), BF16),
             pltpu.VMEM((NT, 64, TW), BF16),
-            dma((17,)),
+            dma((18,)),
             dma((4,)),
             dma((4,)),
             dma((2,)),
@@ -515,7 +519,7 @@
             dma((NT,)),
         ],
         compiler_params=pltpu.CompilerParams(
-            collective_id=0, has_side_effects=True, vmem_limit_bytes=60 * 2**20
+            collective_id=0, has_side_effects=True, vmem_limit_bytes=50 * 2**20
         ),
     )(
         seg_lengths,

time: 52.7 us -> 50.7 us (0.962)
  Pallas kernels: 50.3 us -> 48.7 us
    pallas_call x1, Pallas kernels: 50.3 us -> 48.7 us  [body(): pl.pallas_call(kernel, out_shape=jax.ShapeDtypeStruct((64, D), BF16), in_...]
    unnamed x1 -> x3, local copies, waits for them, and re-layouts: 1.87 us -> 1.45 us
where the time goes in v3:
time: 50.7 us; the launch traced here: 50.2 us
  Pallas kernels  48.7 us (96%)
  local copies, waits for them, and re-layouts  1.45 us (3%)
    pallas_call x1, Pallas kernels, body(): pl.pallas_call(kernel, out_shape=jax.ShapeDtypeStruct((64, D), BF16), in_...  48.7 us
    unnamed x3, local copies, waits for them, and re-layouts  1.45 us

profile of v3, /device:TPU:0, one launch (start us, length us, event | category | flops | bytes accessed | tf_op | source)
XLA Modules:
  0.0 50.2 jit_solution(6159584708321466638)
XLA Ops:
  0.0 0.0 copy-start
  0.0 0.7 %copy-done = s32[16]{0:T(128)S(1)} copy-done((s32[16]{0:T(128)S(1)}, s32[16]{0:T(128)}, u32[]{:S(2)}) %copy-start) | copy-done | bytes 88
  0.7 48.7 %shard_map.73 = bf16[64,4096]{1,0:T(8,128)(2,1)S(1)} custom-call(s32[16]{0:T(128)S(1)} %copy-done, bf16[1,512,4096]{2,1,0:T(8,128)(2,1)} %x_hbm.1, bf16[1,512,4096]{2,1,0:T(8,128)(2,1)} %mem_hbm.1, bf16[4096,512]{1,0:T(8,128)(2,1)} %wq_hbm.1, bf16[4096,512]{1,0:T(8,128)(2,1)} %wk_hbm.1, bf16[4096,512]{1,0:T(8,128)(2,1)} %wv_hbm.1, bf16[512,4096]{1,0:T(8,128)(2,1)} %wo_hbm.1), custom_call_target="tpu_custom_call" | custom-call | tf_op jit(solution)/shard_map/pallas_call | solution.py:481
  49.4 0.8 %copy.9 = bf16[1,64,4096]{2,1,0:T(8,128)(2,1)} copy(bf16[1,64,4096]{2,1,0:T(8,128)(2,1)S(1)} %bitcast.1) | data formatting | bytes 1048576
Async XLA Ops:
  0.0 0.7 %copy-start = (s32[16]{0:T(128)S(1)}, s32[16]{0:T(128)}, u32[]{:S(2)}) copy-start(s32[16]{0:T(128)} %lens_hbm.1) | copy-start | bytes 196

commit v4 on v3

--- a/solution.py
+++ b/solution.py
@@ -17,7 +17,7 @@
 HD = 128
 COLS = 512
 PAIR = 256
-PART = 1024
+PART = 2048
 TW = 512
 NT = D // TW
 SCALE = math.log2(math.e) / math.sqrt(HD)
@@ -91,6 +91,38 @@
     def along_x(by):
         return at(s, lax.rem(x + by + 4, 4) * 2 + yh)
 
+    def load_w(src, pair, kind, part, depth, sem):
+        rows = pl.ds(part * depth, depth)
+        return pltpu.make_async_copy(
+            src.at[rows, pl.ds(pair * PAIR, PAIR)],
+            w_v.at[pair, rows, pl.ds(kind * PAIR, PAIR)],
+            ld_sem.at[sem],
+        )
+
+    def first_loads(i):
+        part = pl.ds(pl.multiple_of(i * PART, PART), PART)
+        return (
+            pltpu.make_async_copy(
+                mem_hbm.at[0, :, part], states.at[0, :, part], ld_sem.at[i]
+            ),
+            load_w(wk_hbm, 0, 0, i, PART, 4 + i),
+        )
+
+    load_v0 = load_w(wv_hbm, 0, 1, 0, D, 8)
+
+    load_kv1 = (
+        load_w(wk_hbm, 1, 0, 0, D, 12),
+        load_w(wv_hbm, 1, 1, 0, D, 13),
+    )
+    load_lens = pltpu.make_async_copy(lens_hbm, lens, ld_sem.at[17])
+    load_x = pltpu.make_async_copy(x_hbm.at[0], states.at[1], ld_sem.at[14])
+    load_q = pltpu.make_async_copy(wq_hbm, w_v.at[2], ld_sem.at[15])
+    load_wo = pltpu.make_async_copy(wo_hbm, wo_v, ld_sem.at[16])
+    for i in range(2):
+        for copy in first_loads(i):
+            copy.start()
+    load_lens.start()
+
     barrier = pltpu.get_barrier_semaphore()
     for peer in (
         following,
@@ -104,38 +136,6 @@
     ):
         pl.semaphore_signal(barrier, inc=1, device_id=peer, device_id_type=MESH)
 
-    def load_w(src, pair, kind, part, depth, sem):
-        rows = pl.ds(part * depth, depth)
-        return pltpu.make_async_copy(
-            src.at[rows, pl.ds(pair * PAIR, PAIR)],
-            w_v.at[pair, rows, pl.ds(kind * PAIR, PAIR)],
-            ld_sem.at[sem],
-        )
-
-    def first_loads(i):
-        part = pl.ds(pl.multiple_of(i * PART, PART), PART)
-        return (
-            pltpu.make_async_copy(
-                mem_hbm.at[0, :, part], states.at[0, :, part], ld_sem.at[i]
-            ),
-            load_w(wk_hbm, 0, 0, i, PART, 4 + i),
-        )
-
-    load_v0 = load_w(wv_hbm, 0, 1, 0, D, 8)
-
-    load_kv1 = (
-        load_w(wk_hbm, 1, 0, 0, D, 12),
-        load_w(wv_hbm, 1, 1, 0, D, 13),
-    )
-    load_lens = pltpu.make_async_copy(lens_hbm, lens, ld_sem.at[17])
-    load_x = pltpu.make_async_copy(x_hbm.at[0], states.at[1], ld_sem.at[14])
-    load_q = pltpu.make_async_copy(wq_hbm, w_v.at[2], ld_sem.at[15])
-    load_wo = pltpu.make_async_copy(wo_hbm, wo_v, ld_sem.at[16])
-    for i in range(2):
-        for copy in first_loads(i):
-            copy.start()
-    load_lens.start()
-
     def remote(src, dst, send, recv, to):
         return pltpu.make_async_remote_copy(
             src_ref=src,
@@ -177,9 +177,6 @@
         g = tile(z + (0, 1, -1, 2)[i], cc)
         return remote(wof.at[g], wof.at[g], wbs.at[i], wbr.at[i], sibling)
 
-    load_lens.wait()
-    own_len = lens[s]
-    mem_len = lens[lax.rem(s + 15, 16)]
 
     def row_start(d, which):
         return (lax.rem(x + d, 4) * 2 + which) * 64
@@ -195,9 +192,11 @@
             [lax.broadcasted_iota(jnp.int32, (64, 1), 0) + start for start in starts],
             axis=0,
         )
-        last = jnp.minimum(ids, own_len - 1)
         col = lax.broadcasted_iota(jnp.int32, (1, SEG), 1)
         ones = jnp.ones((SEG, HD), BF16)
+        own_len = lens[s]
+        mem_len = lens[lax.rem(s + 15, 16)]
+        last = jnp.minimum(ids, own_len - 1)
         for pair, hh in [(pair, hh) for pair in pairs for hh in range(2)]:
             ks = slice(hh * HD, (hh + 1) * HD)
             vs = slice(PAIR + hh * HD, PAIR + (hh + 1) * HD)
@@ -234,24 +233,19 @@
         )
 
     def first_part(i, _):
-        c = i // 4
-        n = lax.rem(i, 4)
-
-        @pl.when(i < 4)
+        c = i // 2
+        n = lax.rem(i, 2)
+
+        @pl.when(i < 2)
         def _():
             for copy in first_loads(n):
                 copy.wait()
 
-        @pl.when(i < 2)
-        def _():
-            for copy in first_loads(n + 2):
-                copy.start()
+        @pl.when(i == 0)
+        def _():
+            load_v0.start()
 
         @pl.when(i == 2)
-        def _():
-            load_v0.start()
-
-        @pl.when(i == 4)
         def _():
             load_v0.wait()
             load_kv1[0].start()
@@ -271,26 +265,26 @@
         def _():
             first[...] += term
 
-        @pl.when(n == 3)
+        @pl.when(n == 1)
         def _():
             kv_send[c] = first[...].astype(BF16)
 
-        @pl.when(i == 3)
+        @pl.when(i == 1)
         def _():
             pl.semaphore_wait(barrier, 8)
 
-        @pl.when(n == 3)
+        @pl.when(n == 1)
         def _():
             kv_copy(c).start()
 
-        @pl.when(i == 3)
+        @pl.when(i == 1)
         def _():
             cross_copy(0).start()
             cross_copy(1).start()
 
         return 0
 
-    lax.fori_loop(0, 8, first_part, 0)
+    lax.fori_loop(0, 4, first_part, 0)
 
     def make(i, _):
         own_part = jnp.minimum(i // 2, 1)
@@ -343,6 +337,7 @@
         ctx_copy(ph).start()
         return 0
 
+    load_lens.wait()
     lax.fori_loop(0, 2, phase, 0)
     cross_copy(3).start()
     attend((0, 1), 1)
@@ -419,6 +414,10 @@
         ).astype(BF16)
 
     def out_step(k, _):
+        @pl.when(k >= 3)
+        def _():
+            combine(k - 3)
+
         for j in range(4):
 
             @pl.when(k == 2 * j)
@@ -443,13 +442,9 @@
         def _():
             project_tile(k)
 
-        @pl.when(k >= 4)
-        def _():
-            combine(k - 4)
-
-        return 0
-
-    lax.fori_loop(0, NT + 4, out_step, 0)
+        return 0
+
+    lax.fori_loop(0, NT + 3, out_step, 0)
 
     def last_step(k, _):
         finish(k)

time: 50.7 us -> 50.1 us (0.988)
  no operation moved by 1% of the time
where the time goes in v4:
time: 50.1 us; the launch traced here: 50 us
  Pallas kernels  48.6 us (97%)
  local copies, waits for them, and re-layouts  1.45 us (3%)
    pallas_call x1, Pallas kernels, body(): pl.pallas_call(kernel, out_shape=jax.ShapeDtypeStruct((64, D), BF16), in_...  48.6 us
    unnamed x3, local copies, waits for them, and re-layouts  1.45 us

profile of v4, /device:TPU:0, one launch (start us, length us, event | category | flops | bytes accessed | tf_op | source)
XLA Modules:
  0.0 50.0 jit_solution(66052469610967875)
XLA Ops:
  0.0 0.0 copy-start
  0.0 0.7 %copy-done = s32[16]{0:T(128)S(1)} copy-done((s32[16]{0:T(128)S(1)}, s32[16]{0:T(128)}, u32[]{:S(2)}) %copy-start) | copy-done | bytes 88
  0.7 48.6 %shard_map.73 = bf16[64,4096]{1,0:T(8,128)(2,1)S(1)} custom-call(s32[16]{0:T(128)S(1)} %copy-done, bf16[1,512,4096]{2,1,0:T(8,128)(2,1)} %x_hbm.1, bf16[1,512,4096]{2,1,0:T(8,128)(2,1)} %mem_hbm.1, bf16[4096,512]{1,0:T(8,128)(2,1)} %wq_hbm.1, bf16[4096,512]{1,0:T(8,128)(2,1)} %wk_hbm.1, bf16[4096,512]{1,0:T(8,128)(2,1)} %wv_hbm.1, bf16[512,4096]{1,0:T(8,128)(2,1)} %wo_hbm.1), custom_call_target="tpu_custom_call" | custom-call | tf_op jit(solution)/shard_map/pallas_call | solution.py:476
  49.2 0.8 %copy.9 = bf16[1,64,4096]{2,1,0:T(8,128)(2,1)} copy(bf16[1,64,4096]{2,1,0:T(8,128)(2,1)S(1)} %bitcast.1) | data formatting | bytes 1048576
Async XLA Ops:
  0.0 0.7 %copy-start = (s32[16]{0:T(128)S(1)}, s32[16]{0:T(128)}, u32[]{:S(2)}) copy-start(s32[16]{0:T(128)} %lens_hbm.1) | copy-start | bytes 196

commit v5 on v4

--- a/solution.py
+++ b/solution.py
@@ -313,7 +313,7 @@
                 kv_send[2 + c] = made[1, :, c * PAIR : (c + 1) * PAIR]
                 kv_copy(2 + c).start()
 
-        @pl.when(i == 3)
+        @pl.when(i == 2)
         def _():
             cross_copy(0).wait_recv()
             z_copy(1, 0, z).start()

time: 50.1 us -> 50.1 us (level)
  no operation moved by 1% of the time
where the time goes in v5:
time: 50.1 us; the launch traced here: 50 us
  Pallas kernels  48.6 us (97%)
  local copies, waits for them, and re-layouts  1.45 us (3%)
    pallas_call x1, Pallas kernels, body(): pl.pallas_call(kernel, out_shape=jax.ShapeDtypeStruct((64, D), BF16), in_...  48.6 us
    unnamed x3, local copies, waits for them, and re-layouts  1.45 us

profile of v5, /device:TPU:0, one launch (start us, length us, event | category | flops | bytes accessed | tf_op | source)
XLA Modules:
  0.0 50.0 jit_solution(3951811400542396747)
XLA Ops:
  0.0 0.0 copy-start
  0.0 0.7 %copy-done = s32[16]{0:T(128)S(1)} copy-done((s32[16]{0:T(128)S(1)}, s32[16]{0:T(128)}, u32[]{:S(2)}) %copy-start) | copy-done | bytes 88
  0.7 48.6 %shard_map.73 = bf16[64,4096]{1,0:T(8,128)(2,1)S(1)} custom-call(s32[16]{0:T(128)S(1)} %copy-done, bf16[1,512,4096]{2,1,0:T(8,128)(2,1)} %x_hbm.1, bf16[1,512,4096]{2,1,0:T(8,128)(2,1)} %mem_hbm.1, bf16[4096,512]{1,0:T(8,128)(2,1)} %wq_hbm.1, bf16[4096,512]{1,0:T(8,128)(2,1)} %wk_hbm.1, bf16[4096,512]{1,0:T(8,128)(2,1)} %wv_hbm.1, bf16[512,4096]{1,0:T(8,128)(2,1)} %wo_hbm.1), custom_call_target="tpu_custom_call" | custom-call | tf_op jit(solution)/shard_map/pallas_call | solution.py:476
  49.2 0.8 %copy.9 = bf16[1,64,4096]{2,1,0:T(8,128)(2,1)} copy(bf16[1,64,4096]{2,1,0:T(8,128)(2,1)S(1)} %bitcast.1) | data formatting | bytes 1048576
Async XLA Ops:
  0.0 0.7 %copy-start = (s32[16]{0:T(128)S(1)}, s32[16]{0:T(128)}, u32[]{:S(2)}) copy-start(s32[16]{0:T(128)} %lens_hbm.1) | copy-start | bytes 196
